TPU v7x, 512 devices: a whole 4x8x8 slice. The times are simulated.
512 devices in a mesh: grp: 16 (over y, core), ep: 32 (over z, x).
Axes of the slice: x: 4, y: 8, z: 8, core: 2. Of those that a mesh axis runs over, the one named last changes fastest.
Arguments:
- resp_q: bfloat16 [65536, 4096], P(('grp', 'ep')), may hold values from -6 to 6
- resp_kv: bfloat16 [65536, 512], P(('grp', 'ep')), may hold values from -96 to 96
- prompt_kv: bfloat16 [12288, 512], P(('grp', 'ep')), may hold values from -96 to 96
- moe_in: bfloat16 [65536, 2048], P(('grp', 'ep')), may hold values from -6 to 6
- routes: int32 [65536, 8], P(('grp', 'ep')), may hold values from 0 to 127, all different within a row; in each aligned block of 128 rows (0 to 127, 128 to 255, ...) at most 16 rows name the same one
- gate_probs: float32 [65536, 8], P(('grp', 'ep')), may hold values from 0.1 to 1
- w_gate: bfloat16 [32, 2048, 768], P('ep', 'grp'), may hold values from -0.125 to 0.125
- w_up: bfloat16 [32, 2048, 768], P('ep', 'grp'), may hold values from -0.125 to 0.125
- w_down: bfloat16 [32, 2048, 768], P('ep', 'grp'), may hold values from -0.21875 to 0.21875
Outputs:
- context: bfloat16 [65536, 4096], P(('grp', 'ep'))
- moe_out: bfloat16 [65536, 2048], P(('grp', 'ep'))
Inputs may be any that keep to these rules, and one draw needn't show every extreme that they name: `routes`: each row names 8 different experts; within the 128 rows of one device no expert is named more than 16 times.
All inputs are finite; a program needn't handle non-finite values.
Results may differ from a plain program's by a relative error of at most 0.0057.
Values may be sent and summed in bfloat16 or wider, within the bound.
A program may use at most 64 MiB of HBM per device.

v0:
```python
import jax
import jax.numpy as jnp
from jax import lax
from jax.sharding import PartitionSpec as P

D = 2048
HQ = 32
KVH = 2
HD = 128
EXPERTS = 128
TOPK = 8
CAP = 16


def head_context(
    query_head, prompt_keys_rows, prompt_values_rows, resp_keys_rows, resp_values_rows, resp_visible
):
    score_scale = HD ** (-0.5)
    token_count = query_head.shape[0]
    all_keys = jnp.concatenate([prompt_keys_rows, resp_keys_rows], axis=0)
    all_values = jnp.concatenate([prompt_values_rows, resp_values_rows], axis=0)
    prompt_visible = jnp.ones((token_count, prompt_keys_rows.shape[0]), jnp.bool_)
    visible = jnp.concatenate([prompt_visible, resp_visible], axis=1)
    scores = (
        jnp.einsum("tgd,kd->tgk", query_head, all_keys, preferred_element_type=jnp.float32)
        * score_scale
    )
    scores = jnp.where(visible[:, None, :], scores, -jnp.inf)
    row_max = jnp.max(scores, axis=-1, keepdims=True)
    exp_scores = jnp.exp(scores - row_max)
    denominator = jnp.sum(exp_scores, axis=-1)
    summed = jnp.einsum(
        "tgk,kd->tgd",
        exp_scores.astype(jnp.bfloat16),
        all_values,
        preferred_element_type=jnp.float32,
    )
    return (summed / denominator[..., None]).astype(jnp.bfloat16)


def attention(resp_q, resp_kv, prompt_kv):
    prompt = lax.all_gather(prompt_kv, "ep", axis=0, tiled=True)
    token_count = resp_q.shape[0]
    lane_width = KVH * HD
    query_pos = jnp.arange(token_count)[:, None]
    own_pos = jnp.arange(token_count)[None, :]
    resp_visible = own_pos <= query_pos
    grouped = resp_q.reshape(token_count, KVH, HQ // KVH, HD)
    results = []
    for head_index in range(KVH):
        offset = head_index * HD
        results.append(
            head_context(
                grouped[:, head_index],
                prompt[:, offset : offset + HD],
                prompt[:, lane_width + offset : lane_width + offset + HD],
                resp_kv[:, offset : offset + HD],
                resp_kv[:, lane_width + offset : lane_width + offset + HD],
                resp_visible,
            )
        )
    return jnp.stack(results, axis=1).reshape(token_count, HQ * HD)


def slot_layout(route_rows, ep_count):
    per_dev = EXPERTS // ep_count
    expert_range = jnp.arange(EXPERTS, dtype=jnp.int32)
    member = (route_rows[:, None] == expert_range[None, :]).astype(jnp.int32)
    earlier = jnp.cumsum(member, axis=0) - member
    position = jnp.sum(earlier * member, axis=1)
    active = route_rows % per_dev == 0
    target = jnp.where(active, route_rows // per_dev * CAP + position, ep_count * CAP)
    return (active, target)


def expert_partial(token_rows, gate_full, up_full, down_full):
    gate_part = jnp.dot(token_rows, gate_full, preferred_element_type=jnp.float32)
    up_part = jnp.dot(token_rows, up_full, preferred_element_type=jnp.float32)
    hidden = (jax.nn.silu(gate_part) * up_part).astype(jnp.bfloat16)
    return lax.dot_general(
        hidden, down_full, (((1,), (1,)), ((), ())), preferred_element_type=jnp.float32
    )


def experts(moe_in, routes, gate_probs, w_gate, w_up, w_down):
    ep_count = lax.axis_size("ep")
    token_count = moe_in.shape[0]
    active, target = slot_layout(routes.reshape(-1), ep_count)
    repeated = jnp.repeat(moe_in, TOPK, axis=0)
    outgoing = jnp.zeros((ep_count * CAP, D), jnp.bfloat16).at[target].set(repeated, mode="drop")
    received = lax.all_to_all(
        outgoing.reshape(ep_count, CAP, D), "ep", split_axis=0, concat_axis=0, tiled=True
    )
    token_rows = received.reshape(ep_count * CAP, D)
    gate_shard = w_gate[0]
    up_shard = w_up[0]
    down_shard = w_down[0]
    full_gate, full_up, full_down = (
        lax.all_gather(gate_shard, "grp", axis=0, tiled=True),
        lax.all_gather(up_shard, "grp", axis=0, tiled=True),
        lax.all_gather(down_shard, "grp", axis=0, tiled=True),
    )
    produced = expert_partial(token_rows, full_gate, full_up, full_down)
    outputs = produced.astype(jnp.bfloat16).reshape(ep_count, CAP, D)
    returned = lax.all_to_all(outputs, "ep", split_axis=0, concat_axis=0, tiled=True).reshape(
        ep_count * CAP, D
    )
    picked = jnp.take(returned, jnp.minimum(target, ep_count * CAP - 1), axis=0)
    weighting = jnp.where(active, gate_probs.reshape(-1), 0.0)
    summed = (picked.astype(jnp.float32) * weighting[:, None]).reshape(token_count, TOPK, D)
    return jnp.sum(summed, axis=1).astype(jnp.bfloat16)


def body(resp_q, resp_kv, prompt_kv, moe_in, routes, gate_probs, w_gate, w_up, w_down):
    context = attention(resp_q, resp_kv, prompt_kv)
    moe_out = experts(moe_in, routes, gate_probs, w_gate, w_up, w_down)
    return (context, moe_out)


def solution(mesh):
    placed = (
        P(("grp", "ep"), None),
        P(("grp", "ep"), None),
        P(("grp", "ep"), None),
        P(("grp", "ep"), None),
        P(("grp", "ep"), None),
        P(("grp", "ep"), None),
        P("ep", "grp", None),
        P("ep", "grp", None),
        P("ep", "grp", None),
    )
    return jax.shard_map(
        body,
        mesh=mesh,
        in_specs=placed,
        out_specs=(P(("grp", "ep"), None), P(("grp", "ep"), None)),
        check_vma=False,
    )
```

profile of v0, /device:TPU:5, one launch (start us, length us, event | category | flops | bytes accessed | tf_op | source)
XLA Modules:
  0.0 235.3 jit_solution(17615579049432805257)
XLA Ops:
  7.2 0.7 all-gather.7.cloned.1.call-update
  8.0 0.7 all-gather.11.cloned.1.call-update
  8.7 0.7 all-gather.9.cloned.1.call-update
  9.4 0.8 copy.25
  11.0 0.4 fusion.42
  11.4 7.9 %scatter_custom_fusion = bf16[512,2048]{1,0:T(8,128)(2,1)} fusion(s32[1024]{0:T(1024)S(1)} %bitcast.110, bf16[128,2048]{1,0:T(8,128)(2,1)S(1)} %copy-done, bf16[]{:T(256)} %constant.66.clone.1), kind=kCustom, calls=%fused_computation.14 | custom fusion | bytes 2621442 | tf_op jit(solution)/shard_map/scatter | solution.py:90
  19.4 13.0 %all-to-all-start = ((bf16[32,16,2048]{2,1,0:T(8,128)(2,1)}), bf16[32,16,2048]{2,1,0:T(8,128)(2,1)S(1)}, u32[]{:S(2)}, u32[]{:S(2)}) async-start(bf16[32,16,2048]{2,1,0:T(8,128)(2,1)} %bitcast.18), calls=%async_computation | async-start | bytes 4194304 | tf_op jit(solution)/shard_map/all_to_all | solution.py:91
  32.5 2.3 copy.18
  34.8 78.1 %all_gather.12 = bf16[768,512]{1,0:T(8,128)(2,1)S(1)} all-gather(bf16[24,512]{1,0:T(8,128)(2,1)S(1)} %copy-done.6), channel_id=1, replica_groups=mesh['grp'=16,'ep'=32] {'ep'}, dimensions={0}, use_global_device_ids=true | all-gather | bytes 811008 | tf_op jit(solution)/shard_map/all_gather | solution.py:42
  112.9 0.7 fusion.71
  113.7 4.9 %fusion.18 = f32[512,768]{1,0:T(8,128)} fusion(bf16[512,2048]{1,0:T(8,128)(2,1)S(1)} %bitcast.106, bf16[1,2048,768]{2,1,0:T(8,128)(2,1)} %all-gather.7.cloned.1.call-done), kind=kOutput, calls=%fused_computation.24 | convolution fusion | flops 1610612736 | bytes 6815744 | tf_op jit(solution)/shard_map/dot_general | solution.py:77
  118.6 29.3 %all-gather.9.cloned.1.call-done = bf16[1,2048,768]{2,1,0:T(8,128)(2,1)} async-done(((bf16[1,128,768]{2,1,0:T(8,128)(2,1)}), bf16[1,2048,768]{2,1,0:T(8,128)(2,1)}) %all-gather.9.cloned.1.call-update) | async-done | bytes 3145744 | tf_op jit(solution)/shard_map/all_gather | solution.py:100
  147.9 8.6 %fusion.20 = bf16[512,2048]{1,0:T(8,128)(2,1)} fusion(bf16[1,2048,768]{2,1,0:T(8,128)(2,1)} %all-gather.11.cloned.1.call-done, f32[512,768]{1,0:T(8,128)} %fusion.18, bf16[512,2048]{1,0:T(8,128)(2,1)S(1)} %bitcast.107, bf16[1,2048,768]{2,1,0:T(8,128)(2,1)} %all-gather.9.cloned.1.call-done), kind=kOutput, calls=%fused_computation.26 | convolution fusion | flops 3224633344 | bytes 12058624 | tf_op jit(solution)/shard_map/dot_general | solution.py:80
  156.5 9.9 %all-to-all-start.1 = ((bf16[32,16,2048]{2,1,0:T(8,128)(2,1)}), bf16[32,16,2048]{2,1,0:T(8,128)(2,1)S(1)}, u32[]{:S(2)}, u32[]{:S(2)}) async-start(bf16[32,16,2048]{2,1,0:T(8,128)(2,1)} %bitcast.105), calls=%async_computation.1 | async-start | bytes 4194304 | tf_op jit(solution)/shard_map/all_to_all | solution.py:105
  166.5 2.3 fusion.4
  168.8 2.8 %fusion = (f32[128,16]{0,1:T(8,128)S(1)}, f32[128,16]{0,1:T(8,128)S(1)}, f32[896,128,16]{1,0,2:T(8,128)S(1)}) fusion(f32[896,128,16]{1,0,2:T(8,128)S(1)} %get-tuple-element.19, f32[128,16]{0,1:T(8,128)S(1)} %get-tuple-element.18, pred[128,896]{0,1:T(8,128)(4,1)S(1)} %concatenate.16, bf16[128,2,16,128]{0,3,2,1:T(8,128)(2,1)S(1)} %bitcast.104, ...), kind=kOutput, calls=%fused_computation.7 | convolution fusion | flops 483061760 | bytes 15572992 | tf_op jit(solution)/shard_map/tgd,kd->tgk/dot_general | solution.py:25
  171.6 1.5 fusion.2
  173.1 1.8 fusion.34
  174.9 1.8 fusion.29
  176.7 1.1 pad_maximum_fusion
  177.8 2.3 copy.35
  180.3 36.2 %all-to-all-done.1 = bf16[32,16,2048]{2,1,0:T(8,128)(2,1)S(1)} async-done(((bf16[32,16,2048]{2,1,0:T(8,128)(2,1)}), bf16[32,16,2048]{2,1,0:T(8,128)(2,1)S(1)}, u32[]{:S(2)}, u32[]{:S(2)}) %all-to-all-start.1) | async-done | bytes 2097184 | tf_op jit(solution)/shard_map/all_to_all | solution.py:105
  216.5 6.0 %gather_fusion = bf16[1024,2048]{1,0:T(8,128)(2,1)} fusion(bf16[512,2048]{1,0:T(8,128)(2,1)S(1)} %bitcast.101, s32[1024]{0:T(1024)S(1)} %broadcast_clamp_fusion), kind=kCustom, calls=%fused_computation | custom fusion | bytes 8392704 | tf_op jit(solution)/shard_map/jit(_take)/gather | solution.py:108
  222.5 6.3 %multiply_reduce_fusion = bf16[128,2048]{1,0:T(8,128)(2,1)} fusion(bf16[1024,2048]{1,0:T(8,128)(2,1)} %gather_fusion, f32[128,8]{1,0:T(8,128)S(1)} %broadcast_select_fusion, pred[128,8]{1,0:T(8,128)(4,1)S(1)} %compare_and_fusion), kind=kLoop, calls=%fused_computation.2 | loop fusion | flops 8126464 | bytes 4723712 | tf_op jit(solution)/shard_map/reduce_sum | solution.py:111
  (42 shorter events, 1.5 us)
Async XLA Ops:
  7.2 4.2 %copy-start = (bf16[128,2048]{1,0:T(8,128)(2,1)S(1)}, bf16[128,2048]{1,0:T(8,128)(2,1)}, u32[]{:S(2)}) copy-start(bf16[128,2048]{1,0:T(8,128)(2,1)} %param.12) | copy-start | bytes 1572868
  7.2 106.5 %all-gather.7.cloned.1.call-start = ((), (), s32[]{:S(2)}) async-start(), calls=%async_computation.2 | async-start | bytes 3342336 | tf_op jit(solution)/shard_map/all_gather | solution.py:99
  7.9 110.7 %all-gather.11.cloned.1.call-start = ((), (), s32[]{:S(2)}) async-start(), calls=%async_computation.4 | async-start | bytes 3342336 | tf_op jit(solution)/shard_map/all_gather | solution.py:101
  8.7 139.2 %all-gather.9.cloned.1.call-start = ((), (), s32[]{:S(2)}) async-start(), calls=%async_computation.3 | async-start | bytes 3342336 | tf_op jit(solution)/shard_map/all_gather | solution.py:100
  11.4 23.3 %copy-start.6 = (bf16[24,512]{1,0:T(8,128)(2,1)S(1)}, bf16[24,512]{1,0:T(8,128)(2,1)}, u32[]{:S(2)}) copy-start(bf16[24,512]{1,0:T(8,128)(2,1)} %param.11) | copy-start | bytes 73732
  19.4 93.5 %copy-start.2 = (bf16[128,512]{1,0:T(8,128)(2,1)S(1)}, bf16[128,512]{1,0:T(8,128)(2,1)}, u32[]{:S(2)}) copy-start(bf16[128,512]{1,0:T(8,128)(2,1)} %param.10) | copy-start | bytes 393220
  19.4 94.3 %all-to-all-start = ((bf16[32,16,2048]{2,1,0:T(8,128)(2,1)}), bf16[32,16,2048]{2,1,0:T(8,128)(2,1)S(1)}, u32[]{:S(2)}, u32[]{:S(2)}) async-start(bf16[32,16,2048]{2,1,0:T(8,128)(2,1)} %bitcast.18), calls=%async_computation | async-start | bytes 4194304 | tf_op jit(solution)/shard_map/all_to_all | solution.py:91
  156.5 60.0 %all-to-all-start.1 = ((bf16[32,16,2048]{2,1,0:T(8,128)(2,1)}), bf16[32,16,2048]{2,1,0:T(8,128)(2,1)S(1)}, u32[]{:S(2)}, u32[]{:S(2)}) async-start(bf16[32,16,2048]{2,1,0:T(8,128)(2,1)} %bitcast.105), calls=%async_computation.1 | async-start | bytes 4194304 | tf_op jit(solution)/shard_map/all_to_all | solution.py:105
  166.4 2.3 copy-start.1
  166.5 2.3 copy-start.5
  171.6 1.5 copy-start.4
  173.1 1.8 copy-start.3
  176.7 3.4 %copy-start.7 = (f32[128,8]{0,1:T(8,128)S(1)}, f32[128,8]{0,1:T(8,128)}, u32[]{:S(2)}) copy-start(f32[128,8]{0,1:T(8,128)} %param.14) | copy-start | bytes 12292
Sparse Core Ops, SparseCore 0:
  10.1 48.5 all-gather.6
  60.8 42.4 all-gather.10
  105.4 42.4 all-gather.8
where the time goes:
time: 236 us; the launch traced here: 235 us
  blocking collectives  78.1 us (33%)
  waiting for transfers between devices  67.6 us (29%)
  starting transfers between devices  23.1 us (10%)
  matrix products  22.1 us (9%)
  local copies, waits for them, and re-layouts  20.8 us (9%)
  between operations  14 us (6%)
  other arithmetic  9.66 us (4%)
    all_gather x1, blocking collectives, attention(): prompt = lax.all_gather(prompt_kv, 'ep', axis=0, tiled=True)  78.1 us
    all_to_all x1, waiting for transfers between devices, experts(): lax.all_to_all(outputs, 'ep', split_axis=0, concat_axis=0, tiled=True)  36.2 us
    all_gather x1, waiting for transfers between devices, experts(): lax.all_gather(up_shard, 'grp', axis=0, tiled=True)  29.3 us
    all_to_all x1, starting transfers between devices, experts(): lax.all_to_all(outgoing.reshape(ep_count, CAP, D), 'ep', split_axis=0, co...  13 us
    all_to_all x1, starting transfers between devices, experts(): lax.all_to_all(outputs, 'ep', split_axis=0, concat_axis=0, tiled=True)  9.95 us
    dot_general x1, matrix products, expert_partial(): lax.dot_general(hidden, down_full, (((1,), (1,)), ((), ())), preferred_el...  8.61 us
    scatter x1, local copies, waits for them, and re-layouts, experts(): jnp.zeros((ep_count * CAP, D), jnp.bfloat16).at[target]  7.93 us
    reduce_sum x1, other arithmetic, experts(): return jnp.sum(summed, axis=1).astype(jnp.bfloat16)  6.27 us
  transfers between devices with their start and end apart: 5, of which 2 were waited for; matrix products, arithmetic and copies ran while one was open for 13% of the time, Pallas kernels for 0%

commit v1 on v0

v1 whole, which is shorter than its diff:
```python
import jax
import jax.numpy as jnp
from jax import lax
from jax.experimental import pallas as pl
from jax.experimental.pallas import tpu as pltpu
from jax.sharding import PartitionSpec as P

D = 2048
FF = 768
HQ = 32
KVH = 2
HD = 128
TOPK = 8
TOK = 128
CAP = 16
EXP_DEV = 4
SHARD = 128
PROMPT_ROWS = 24
NX, NY, NZ = 4, 8, 8
NEP = NX * NZ
SLOTS = NEP * CAP
HALF = SLOTS // 2
MESH = pl.DeviceIdType.MESH
SCALE = HD ** -0.5


def layer_kernel(
    q_hbm, resp_kv, prompt_kv, moe_in, routes_t, gates_t, wg_hbm, wu_hbm, wd_hbm,
    ctx_hbm, moe_out,
    weights, outgoing, received, hidden, produced, returned, gate_hi, gate_lo,
    q_buf, ctx_buf, prompt_buf, keys, values,
    local_sem, ring_send, ring_recv, sib_send, sib_recv, pz_send, pz_recv, px_send, px_recv,
    disp_send, disp_recv, ret_send, ret_recv,
):
    grp = lax.axis_index("grp")
    ep = lax.axis_index("ep")
    y, core = grp // 2, grp % 2
    z, x = ep // NX, ep % NX
    sibling = y * 2 + (1 - core)
    right = ((y + 1) % NY) * 2 + core
    left = ((y + NY - 1) % NY) * 2 + core
    shards = (wg_hbm, wu_hbm, wd_hbm)

    barrier = pltpu.get_barrier_semaphore()
    for other in (sibling, right, left):
        pl.semaphore_signal(barrier, inc=1, device_id=(other, ep), device_id_type=MESH)

    @pl.loop(1, NEP)
    def _(d):
        pl.semaphore_signal(barrier, inc=1, device_id=(grp, (ep + d) % NEP), device_id_type=MESH)

    def own_rows(origin):
        return pl.ds(pl.multiple_of(origin * SHARD, SHARD), SHARD)

    q_copy = pltpu.make_async_copy(q_hbm, q_buf, local_sem.at[0])
    q_copy.start()
    own_copies = [
        pltpu.make_async_copy(shards[m], weights.at[m, own_rows(grp), :], local_sem.at[1 + m])
        for m in range(3)
    ]
    for copy in own_copies:
        copy.start()

    rows = prompt_kv[...].astype(jnp.float32)
    prompt_buf[x, z] = jnp.concatenate(
        [rows[:, : KVH * HD], rows[:, KVH * HD :]], axis=0
    ).astype(jnp.bfloat16)

    owner_expert = lax.broadcasted_iota(jnp.int32, (NEP, TOK), 0) * EXP_DEV
    member = jnp.zeros((NEP, TOK), jnp.float32)
    gate = jnp.zeros((NEP, TOK), jnp.float32)
    for k in range(TOPK):
        hit = routes_t[k : k + 1, :] == owner_expert
        member = member + jnp.where(hit, 1.0, 0.0)
        gate = gate + jnp.where(hit, gates_t[k : k + 1, :], 0.0)
    earlier = lax.broadcasted_iota(jnp.int32, (TOK, TOK), 0) < lax.broadcasted_iota(
        jnp.int32, (TOK, TOK), 1
    )
    position = jnp.dot(
        member.astype(jnp.bfloat16),
        jnp.where(earlier, 1.0, 0.0).astype(jnp.bfloat16),
        preferred_element_type=jnp.float32,
    )
    position = jnp.where(member > 0.0, position, -1.0)
    slot = lax.broadcasted_iota(jnp.int32, (NEP, CAP, TOK), 1).astype(jnp.float32)
    taken = jnp.broadcast_to(position[:, None, :], (NEP, CAP, TOK)) == slot
    onehot = jnp.where(taken, 1.0, 0.0).reshape(SLOTS, TOK).astype(jnp.bfloat16)
    for n in range(D // 256):
        outgoing[:, n * 256 : (n + 1) * 256] = jnp.dot(
            onehot, moe_in[:, n * 256 : (n + 1) * 256], preferred_element_type=jnp.float32
        ).astype(jnp.bfloat16)

    pl.semaphore_wait(barrier, NEP + 2)

    def ring_copy(direction, step, m):
        target = right if direction == 0 else left
        origin = ((y + NY - (step - 1)) % NY if direction == 0 else (y + step - 1) % NY) * 2 + core
        if step == NY // 2:
            start = pl.multiple_of(origin * SHARD + direction * (SHARD // 2), SHARD // 2)
            span = pl.ds(start, SHARD // 2)
        else:
            span = own_rows(origin)
        dst = weights.at[m, span, :]
        src = shards[m] if step == 1 else dst
        return pltpu.make_async_remote_copy(
            src_ref=src, dst_ref=dst,
            send_sem=ring_send.at[direction, step - 1, m],
            recv_sem=ring_recv.at[direction, step - 1, m],
            device_id=(target, ep), device_id_type=MESH,
        )

    def ring_arrival(direction, step, m):
        origin = ((y + NY - step) % NY if direction == 0 else (y + step) % NY) * 2 + core
        if step == NY // 2:
            start = pl.multiple_of(origin * SHARD + direction * (SHARD // 2), SHARD // 2)
            span = pl.ds(start, SHARD // 2)
        else:
            span = own_rows(origin)
        return weights.at[m, span, :]

    def sib_copy(kind, src, dst, m):
        return pltpu.make_async_remote_copy(
            src_ref=src, dst_ref=dst,
            send_sem=sib_send.at[kind, m], recv_sem=sib_recv.at[kind, m],
            device_id=(sibling, ep), device_id_type=MESH,
        )

    def pz_copy(d):
        return pltpu.make_async_remote_copy(
            src_ref=prompt_buf.at[x, z], dst_ref=prompt_buf.at[x, z],
            send_sem=pz_send.at[d - 1], recv_sem=pz_recv.at[d - 1],
            device_id=(grp, ((z + d) % NZ) * NX + x), device_id_type=MESH,
        )

    def px_copy(d):
        return pltpu.make_async_remote_copy(
            src_ref=prompt_buf.at[x], dst_ref=prompt_buf.at[x],
            send_sem=px_send.at[d - 1], recv_sem=px_recv.at[d - 1],
            device_id=(grp, z * NX + (x + d) % NX), device_id_type=MESH,
        )

    def place(source):
        return pl.ds(pl.multiple_of(((source % NX) * NZ + source // NX) * CAP, CAP), CAP)

    def owner_rows(owner):
        return pl.ds(pl.multiple_of(owner * CAP, CAP), CAP)

    def disp_copy(d):
        owner = (ep + d) % NEP
        return pltpu.make_async_remote_copy(
            src_ref=outgoing.at[owner_rows(owner), :], dst_ref=received.at[place(ep), :],
            send_sem=disp_send.at[d], recv_sem=disp_recv.at[d],
            device_id=(grp, owner), device_id_type=MESH,
        )

    def disp_arrival(d):
        source = (ep + NEP - d) % NEP
        return pltpu.make_async_remote_copy(
            src_ref=outgoing.at[owner_rows(source), :], dst_ref=received.at[place(source), :],
            send_sem=disp_send.at[d], recv_sem=disp_recv.at[d],
            device_id=(grp, source), device_id_type=MESH,
        )

    def ret_copy(source):
        d = (source + NEP - ep) % NEP
        return pltpu.make_async_remote_copy(
            src_ref=produced.at[place(source), :], dst_ref=returned.at[owner_rows(ep), :],
            send_sem=ret_send.at[d], recv_sem=ret_recv.at[d],
            device_id=(grp, source), device_id_type=MESH,
        )

    def ret_arrival(d):
        owner = (ep + NEP - d) % NEP
        return pltpu.make_async_remote_copy(
            src_ref=produced.at[place(owner), :], dst_ref=returned.at[owner_rows(owner), :],
            send_sem=ret_send.at[d], recv_sem=ret_recv.at[d],
            device_id=(grp, owner), device_id_type=MESH,
        )

    for d in range(1, NZ):
        pz_copy(d).start()
    for m in range(3):
        for direction in range(2):
            ring_copy(direction, 1, m).start()
    for m in range(3):
        sib_copy(0, shards[m], weights.at[m, own_rows(grp), :], m).start()

    @pl.loop(1, NEP)
    def _(d):
        disp_copy(d).start()

    received[place(ep), :] = outgoing[owner_rows(ep), :]

    spread = jnp.where(taken, jnp.broadcast_to(gate[:, None, :], (NEP, CAP, TOK)), 0.0)
    spread = spread.reshape(SLOTS, TOK).T
    high = spread.astype(jnp.bfloat16)
    gate_hi[...] = high
    gate_lo[...] = (spread - high.astype(jnp.float32)).astype(jnp.bfloat16)

    for d in range(1, NZ):
        pz_copy(d).wait_recv()
    for d in range(1, NX):
        px_copy(d).start()

    def ring_turn(step, m):
        for direction in range(2):
            landed = ring_arrival(direction, step, m)
            pltpu.make_async_remote_copy(
                src_ref=landed, dst_ref=landed,
                send_sem=ring_send.at[direction, step - 1, m],
                recv_sem=ring_recv.at[direction, step - 1, m],
                device_id=(right if direction == 0 else left, ep), device_id_type=MESH,
            ).wait_recv()
            if step < NY // 2:
                ring_copy(direction, step + 1, m).start()
            sib_copy(1 + direction * (NY // 2) + step - 1, landed, landed, m).start()

    def gather_prompt():
        for d in range(1, NX):
            px_copy(d).wait_recv()

        @pl.loop(0, NEP // 2)
        def _(i):
            first = prompt_buf[i // 4, (i % 4) * 2].astype(jnp.float32)
            second = prompt_buf[i // 4, (i % 4) * 2 + 1].astype(jnp.float32)
            at = pl.ds(pl.multiple_of(i * 2 * PROMPT_ROWS, 2 * PROMPT_ROWS), 2 * PROMPT_ROWS)
            keys[at, :] = jnp.concatenate(
                [first[:PROMPT_ROWS], second[:PROMPT_ROWS]], axis=0
            ).astype(jnp.bfloat16)
            values[at, :] = jnp.concatenate(
                [first[PROMPT_ROWS:], second[PROMPT_ROWS:]], axis=0
            ).astype(jnp.bfloat16)

    causal = lax.broadcasted_iota(jnp.int32, (TOK, TOK), 1) <= lax.broadcasted_iota(
        jnp.int32, (TOK, TOK), 0
    )

    def attend(first, last):
        @pl.loop(first, last)
        def _(head):
            at = pl.ds(pl.multiple_of(head * HD, HD), HD)
            kv = pl.ds(pl.multiple_of((head // (HQ // KVH)) * HD, HD), HD)
            kv_value = pl.ds(pl.multiple_of(KVH * HD + (head // (HQ // KVH)) * HD, HD), HD)
            query = q_buf[:, at]
            contract = (((1,), (1,)), ((), ()))
            shared = lax.dot_general(
                query, keys[:, kv], contract, preferred_element_type=jnp.float32
            )
            own = lax.dot_general(
                query, resp_kv[:, kv], contract, preferred_element_type=jnp.float32
            )
            own = jnp.where(causal, own, -jnp.inf)
            top = jnp.maximum(
                jnp.max(shared, axis=-1, keepdims=True), jnp.max(own, axis=-1, keepdims=True)
            )
            shared = jnp.exp((shared - top) * SCALE)
            own = jnp.exp((own - top) * SCALE)
            denominator = jnp.sum(shared, axis=-1, keepdims=True) + jnp.sum(
                own, axis=-1, keepdims=True
            )
            summed = jnp.dot(
                shared.astype(jnp.bfloat16), values[:, kv], preferred_element_type=jnp.float32
            ) + jnp.dot(
                own.astype(jnp.bfloat16), resp_kv[:, kv_value], preferred_element_type=jnp.float32
            )
            ctx_buf[:, at] = (summed / denominator).astype(jnp.bfloat16)

    q_copy.wait()
    ctx_copy = pltpu.make_async_copy(ctx_buf, ctx_hbm, local_sem.at[4])
    ring_turn(1, 0)
    ring_turn(1, 1)
    gather_prompt()
    ring_turn(1, 2)
    attend(0, 4)
    ring_turn(2, 0)
    attend(4, 8)
    ring_turn(2, 1)
    attend(8, 12)
    ring_turn(2, 2)
    attend(12, 16)
    ring_turn(3, 0)
    attend(16, 20)
    ring_turn(3, 1)
    attend(20, 24)
    ring_turn(3, 2)
    attend(24, 28)
    ring_turn(4, 0)
    attend(28, 32)
    ctx_copy.start()
    ring_turn(4, 1)
    ring_turn(4, 2)

    for copy in own_copies:
        copy.wait()
    for m in range(3):
        for kind in range(1 + NY):
            if kind == 0:
                landed = weights.at[m, own_rows(sibling), :]
            else:
                direction, step = (kind - 1) // (NY // 2), (kind - 1) % (NY // 2) + 1
                origin = (
                    (y + NY - step) % NY if direction == 0 else (y + step) % NY
                ) * 2 + (1 - core)
                if step == NY // 2:
                    start = pl.multiple_of(origin * SHARD + direction * (SHARD // 2), SHARD // 2)
                    landed = weights.at[m, pl.ds(start, SHARD // 2), :]
                else:
                    landed = weights.at[m, own_rows(origin), :]
            sib_copy(kind, landed, landed, m).wait_recv()

    @pl.loop(1, NEP)
    def _(d):
        disp_arrival(d).wait_recv()

    for half in range(2):
        span = slice(half * HALF, (half + 1) * HALF)

        @pl.loop(0, FF // 256)
        def _(n):
            at = pl.ds(pl.multiple_of(n * 256, 256), 256)
            gated = jnp.dot(
                received[span, :], weights[0, :, at], preferred_element_type=jnp.float32
            )
            up = jnp.dot(
                received[span, :], weights[1, :, at], preferred_element_type=jnp.float32
            )
            hidden[span, at] = (gated / (1.0 + jnp.exp(-gated)) * up).astype(jnp.bfloat16)

        @pl.loop(0, D // 256)
        def _(n):
            at = pl.ds(pl.multiple_of(n * 256, 256), 256)
            produced[span, at] = lax.dot_general(
                hidden[span, :], weights[2, at, :], (((1,), (1,)), ((), ())),
                preferred_element_type=jnp.float32,
            ).astype(jnp.bfloat16)

        @pl.loop(0, NEP // 2)
        def _(i):
            source = ((z + i) % NZ) * NX + half * 2 + i // NZ

            @pl.when(source != ep)
            def _():
                ret_copy(source).start()

    returned[owner_rows(ep), :] = produced[place(ep), :]

    @pl.loop(1, NEP)
    def _(d):
        ret_arrival(d).wait_recv()

    for n in range(D // 256):
        at = slice(n * 256, (n + 1) * 256)
        moe_out[:, at] = (
            jnp.dot(gate_hi[...], returned[:, at], preferred_element_type=jnp.float32)
            + jnp.dot(gate_lo[...], returned[:, at], preferred_element_type=jnp.float32)
        ).astype(jnp.bfloat16)

    ctx_copy.wait()
    for m in range(3):
        for direction in range(2):
            for step in range(1, NY // 2 + 1):
                ring_copy(direction, step, m).wait_send()
        for kind in range(1 + NY):
            if kind == 0:
                sent = weights.at[m, own_rows(grp), :]
            else:
                sent = ring_arrival((kind - 1) // (NY // 2), (kind - 1) % (NY // 2) + 1, m)
            sib_copy(kind, sent, sent, m).wait_send()
    for d in range(1, NZ):
        pz_copy(d).wait_send()
    for d in range(1, NX):
        px_copy(d).wait_send()

    @pl.loop(1, NEP)
    def _(d):
        disp_copy(d).wait_send()
        ret_arrival(d).wait_send()


def body(resp_q, resp_kv, prompt_kv, moe_in, routes, gate_probs, w_gate, w_up, w_down):
    vmem = pl.BlockSpec(memory_space=pltpu.VMEM)
    anywhere = pl.BlockSpec(memory_space=pl.ANY)
    bf16 = jnp.bfloat16
    dma = pltpu.SemaphoreType.DMA
    return pl.pallas_call(
        layer_kernel,
        out_shape=(
            jax.ShapeDtypeStruct((TOK, HQ * HD), bf16),
            jax.ShapeDtypeStruct((TOK, D), bf16),
        ),
        in_specs=[anywhere] + [vmem] * 5 + [anywhere] * 3,
        out_specs=(anywhere, vmem),
        scratch_shapes=[
            pltpu.VMEM((3, D, FF), bf16),
            pltpu.VMEM((SLOTS, D), bf16),
            pltpu.VMEM((SLOTS, D), bf16),
            pltpu.VMEM((SLOTS, FF), bf16),
            pltpu.VMEM((SLOTS, D), bf16),
            pltpu.VMEM((SLOTS, D), bf16),
            pltpu.VMEM((TOK, SLOTS), bf16),
            pltpu.VMEM((TOK, SLOTS), bf16),
            pltpu.VMEM((TOK, HQ * HD), bf16),
            pltpu.VMEM((TOK, HQ * HD), bf16),
            pltpu.VMEM((NX, NZ, 2 * PROMPT_ROWS, KVH * HD), bf16),
            pltpu.VMEM((NEP * PROMPT_ROWS, KVH * HD), bf16),
            pltpu.VMEM((NEP * PROMPT_ROWS, KVH * HD), bf16),
            dma((5,)),
            dma((2, NY // 2, 3)),
            dma((2, NY // 2, 3)),
            dma((1 + NY, 3)),
            dma((1 + NY, 3)),
            dma((NZ - 1,)),
            dma((NZ - 1,)),
            dma((NX - 1,)),
            dma((NX - 1,)),
            dma((NEP,)),
            dma((NEP,)),
            dma((NEP,)),
            dma((NEP,)),
        ],
        compiler_params=pltpu.CompilerParams(
            collective_id=0, has_side_effects=True, vmem_limit_bytes=48 * 1024 * 1024
        ),
        cost_estimate=pl.CostEstimate(
            flops=7_000_000_000, bytes_accessed=6_000_000, transcendentals=4_000_000
        ),
    )(
        resp_q, resp_kv, prompt_kv, moe_in, routes.T, gate_probs.T,
        w_gate[0], w_up[0], w_down[0],
    )


def solution(mesh):
    placed = P(("grp", "ep"), None)
    weight = P("ep", "grp", None)
    return jax.shard_map(
        body,
        mesh=mesh,
        in_specs=(placed,) * 6 + (weight,) * 3,
        out_specs=(placed, placed),
        check_vma=False,
    )
```

time: 236 us -> 138 us (0.58)
  the two profiles are of different devices: /device:TPU:5 before, /device:TPU:390 now
where the time goes in v1:
time: 138 us
  Pallas kernels  128 us (93%)
  local copies, waits for them, and re-layouts  9.14 us (7%)
    pallas_call x1, Pallas kernels, body(): pl.pallas_call(layer_kernel, out_shape=(jax.ShapeDtypeStruct((TOK, HQ * H...  128 us
    unnamed x20, local copies, waits for them, and re-layouts  9.14 us

profile of v1, /device:TPU:390, one launch (start us, length us, event | category | flops | bytes accessed | tf_op | source)
XLA Modules:
  0.0 138.1 jit_solution(16860851054328888789)
XLA Ops:
  0.6 0.0 copy-start.8
  0.6 0.0 copy-start.7
  0.7 0.7 copy-done.8
  1.3 0.0 copy-done.7
  1.3 0.0 copy-start
  1.3 1.2 copy-done
  2.6 0.0 copy-start.1
  2.6 1.0 copy-done.1
  3.6 0.0 copy-start.2
  3.6 0.9 copy-done.2
  4.5 0.0 copy-start.3
  4.5 0.9 copy-done.3
  5.5 0.0 copy-start.4
  5.5 0.9 copy-done.4
  6.4 0.0 copy-start.5
  6.4 0.9 copy-done.5
  7.3 0.0 copy-start.6
  7.3 0.7 copy-done.6
  8.0 128.3 %shard_map.104 = (bf16[128,4096]{1,0:T(8,128)(2,1)S(1)}, bf16[128,2048]{1,0:T(8,128)(2,1)S(1)}) custom-call(bf16[128,4096]{1,0:T(8,128)(2,1)S(1)} %copy-done, bf16[128,512]{1,0:T(8,128)(2,1)S(1)} %copy-done.5, bf16[24,512]{1,0:T(8,128)(2,1)S(1)} %copy-done.6, bf16[128,2048]{1,0:T(8,128)(2,1)S(1)} %copy-done.1, s32[8,128]{1,0:T(8,128)S(1)} %bitcast.8, ...), custom_call_target="tpu_custom_call" | custom-call | flops 7000000000 | bytes 6000000 | tf_op jit(solution)/shard_map/pallas_call | solution.py:385
  136.3 1.0 copy.13
  137.3 0.8 copy.14
Async XLA Ops:
  0.6 0.7 copy-start.8
  0.6 0.7 copy-start.7
  1.3 1.2 copy-start
  2.6 1.0 copy-start.1
  3.6 0.9 copy-start.2
  4.5 0.9 copy-start.3
  5.5 0.9 copy-start.4
  6.4 0.9 copy-start.5
  7.3 0.7 copy-start.6

commit v2 on v0

v2 whole, which is shorter than its diff:
```python
import jax
import jax.numpy as jnp
from jax import lax
from jax.experimental import pallas as pl
from jax.experimental.pallas import tpu as pltpu
from jax.sharding import PartitionSpec as P

D = 2048
FF = 768
HQ = 32
KVH = 2
HD = 128
TOPK = 8
TOK = 128
CAP = 16
EXP_DEV = 4
SHARD = 128
PROMPT_ROWS = 24
NX, NY, NZ = 4, 8, 8
NEP = NX * NZ
SLOTS = NEP * CAP
HALF = SLOTS // 2
MESH = pl.DeviceIdType.MESH
SCALE = HD ** -0.5
VMEM_LIMIT = 62 * 1024 * 1024


OFFSETS = [divmod(d, NX) for i in range(1, NEP // 2) for d in (i, NEP - i)] + [(NZ // 2, 0)]
Z_ORDER = (1, 7, 2, 6, 3, 5, 4, 0)
X_ORDER = (0, 2, 1, 3)
Y_ORDER = (0, 1, 7, 2, 6, 3, 5, 4)
GROUPS = ((0, 5), (5, 8))


def layer_kernel(
    q_hbm, resp_hbm, prompt_hbm, moe_hbm, routes_hbm, gates_hbm, wg_hbm, wu_hbm, wd_hbm,
    ctx_hbm, moe_out,
    weights, outgoing, received, hidden, produced, returned, gate_hi, gate_lo,
    q_buf, ctx_buf, prompt_buf, keys, values, resp_kv, prompt_kv, moe_in, routes_t, gates_t,
    local_sem, ring_send, ring_recv, sib_send, sib_recv, pz_send, pz_recv, px_send, px_recv,
    disp_send, disp_recv, ret_send, ret_recv,
):
    grp = lax.axis_index("grp")
    ep = lax.axis_index("ep")
    y, core = lax.div(grp, 2), lax.rem(grp, 2)
    z, x = lax.div(ep, NX), lax.rem(ep, NX)
    zs = [lax.rem(z + i, NZ) for i in range(NZ)]
    xs = [lax.rem(x + i, NX) for i in range(NX)]
    ys = [lax.rem(y + i, NY) for i in range(NY)]
    sibling = y * 2 + (1 - core)
    right = ys[1] * 2 + core
    left = ys[NY - 1] * 2 + core
    shards = (wg_hbm, wu_hbm, wd_hbm)

    def in_plane(dz, dx):
        return (grp, zs[dz] * NX + xs[dx])

    loads = [
        pltpu.make_async_copy(src, dst, local_sem.at[i])
        for i, (src, dst) in enumerate(
            [
                (routes_hbm, routes_t), (moe_hbm, moe_in), (prompt_hbm, prompt_kv),
                (gates_hbm, gates_t), (q_hbm, q_buf), (resp_hbm, resp_kv),
            ]
            + [(shards[m], weights.at[m, pl.ds(grp * SHARD, SHARD), :]) for m in range(3)]
        )
    ]
    for load in loads[:4]:
        load.start()

    barrier = pltpu.get_barrier_semaphore()
    for other in (sibling, right, left):
        pl.semaphore_signal(barrier, inc=1, device_id=(other, ep), device_id_type=MESH)
    for dz, dx in OFFSETS:
        pl.semaphore_signal(barrier, inc=1, device_id=in_plane(dz, dx), device_id_type=MESH)
    for load in loads[4:]:
        load.start()

    def shard_rows(origin):
        return pl.ds(pl.multiple_of(origin * SHARD, SHARD), SHARD)

    def ring_span(direction, step, m, of_core):
        origin = ys[(-step if direction == 0 else step) % NY] * 2 + of_core
        if step == NY // 2:
            start = pl.multiple_of(origin * SHARD + direction * (SHARD // 2), SHARD // 2)
            return weights.at[m, pl.ds(start, SHARD // 2), :]
        return weights.at[m, shard_rows(origin), :]

    def ring_copy(direction, step, m):
        dst = ring_span(direction, step - 1, m, core)
        if step == NY // 2:
            origin = ys[(1 - step if direction == 0 else step - 1) % NY] * 2 + core
            start = pl.multiple_of(origin * SHARD + direction * (SHARD // 2), SHARD // 2)
            dst = weights.at[m, pl.ds(start, SHARD // 2), :]
        return pltpu.make_async_remote_copy(
            src_ref=shards[m] if step == 1 else dst, dst_ref=dst,
            send_sem=ring_send.at[direction, step - 1, m],
            recv_sem=ring_recv.at[direction, step - 1, m],
            device_id=(right if direction == 0 else left, ep), device_id_type=MESH,
        )

    def ring_arrival(direction, step, m):
        landed = ring_span(direction, step, m, core)
        return pltpu.make_async_remote_copy(
            src_ref=landed, dst_ref=landed,
            send_sem=ring_send.at[direction, step - 1, m],
            recv_sem=ring_recv.at[direction, step - 1, m],
            device_id=(right if direction == 0 else left, ep), device_id_type=MESH,
        )

    def sib_copy(kind, m, of_core):
        if kind == 0:
            span = weights.at[m, shard_rows(y * 2 + of_core), :]
        else:
            span = ring_span((kind - 1) // (NY // 2), (kind - 1) % (NY // 2) + 1, m, of_core)
        return pltpu.make_async_remote_copy(
            src_ref=shards[m] if kind == 0 else span, dst_ref=span,
            send_sem=sib_send.at[kind, m], recv_sem=sib_recv.at[kind, m],
            device_id=(sibling, ep), device_id_type=MESH,
        )

    def pz_copy(d, arrives=False):
        block = prompt_buf.at[x, zs[-d % NZ] if arrives else z]
        return pltpu.make_async_remote_copy(
            src_ref=block, dst_ref=block, send_sem=pz_send.at[d - 1], recv_sem=pz_recv.at[d - 1],
            device_id=in_plane(d, 0), device_id_type=MESH,
        )

    def px_copy(d, arrives=False):
        block = prompt_buf.at[xs[-d % NX] if arrives else x]
        return pltpu.make_async_remote_copy(
            src_ref=block, dst_ref=block, send_sem=px_send.at[d - 1], recv_sem=px_recv.at[d - 1],
            device_id=in_plane(0, d), device_id_type=MESH,
        )

    def slots_of(dz, dx):
        at = (dz * NX + dx) * CAP
        return slice(at, at + CAP)

    def place_of(dz, dx):
        at = (X_ORDER.index(dx) * NZ + dz) * CAP
        return slice(at, at + CAP)

    def disp_copy(dz, dx):
        k = dz * NX + dx
        return pltpu.make_async_remote_copy(
            src_ref=outgoing.at[slots_of(dz, dx), :],
            dst_ref=received.at[place_of(-dz % NZ, -dx % NX), :],
            send_sem=disp_send.at[k], recv_sem=disp_recv.at[k],
            device_id=in_plane(dz, dx), device_id_type=MESH,
        )

    def ret_copy(dz, dx, group):
        k = dz * NX + dx
        columns = slice(256 * GROUPS[group][0], 256 * GROUPS[group][1])
        return pltpu.make_async_remote_copy(
            src_ref=produced.at[place_of(dz, dx), columns],
            dst_ref=returned.at[slots_of(-dz % NZ, -dx % NX), columns],
            send_sem=ret_send.at[group, k], recv_sem=ret_recv.at[group, k],
            device_id=in_plane(dz, dx), device_id_type=MESH,
        )

    row = lax.broadcasted_iota(jnp.int32, (NEP, TOK), 0)
    owner_z, owner_x = (z + row // NX) % NZ, (x + row % NX) % NX
    owner_expert = (owner_z * NX + owner_x) * EXP_DEV
    loads[0].wait()
    member = jnp.zeros((NEP, TOK), jnp.float32)
    for k in range(TOPK):
        member = member + jnp.where(routes_t[k : k + 1, :] == owner_expert, 1.0, 0.0)
    earlier = lax.broadcasted_iota(jnp.int32, (TOK, TOK), 0) < lax.broadcasted_iota(
        jnp.int32, (TOK, TOK), 1
    )
    position = jnp.dot(
        member.astype(jnp.bfloat16),
        jnp.where(earlier, 1.0, 0.0).astype(jnp.bfloat16),
        preferred_element_type=jnp.float32,
    )
    position = jnp.where(member > 0.0, position, -1.0)
    slot = lax.broadcasted_iota(jnp.int32, (NEP, CAP, TOK), 1).astype(jnp.float32)
    taken = jnp.broadcast_to(position[:, None, :], (NEP, CAP, TOK)) == slot
    onehot = jnp.where(taken, 1.0, 0.0).reshape(SLOTS, TOK).astype(jnp.bfloat16)
    loads[1].wait()
    for n in range(D // 256):
        outgoing[:, n * 256 : (n + 1) * 256] = jnp.dot(
            onehot, moe_in[:, n * 256 : (n + 1) * 256], preferred_element_type=jnp.float32
        ).astype(jnp.bfloat16)

    loads[2].wait()
    rows = prompt_kv[...].astype(jnp.float32)
    prompt_buf[x, z] = jnp.concatenate(
        [rows[:, : KVH * HD], rows[:, KVH * HD :]], axis=0
    ).astype(jnp.bfloat16)

    pl.semaphore_wait(barrier, NEP + 2)
    for m in range(2):
        for direction in range(2):
            ring_copy(direction, 1, m).start()
    for d in range(1, NZ):
        pz_copy(d).start()
    for half in range(2):
        for dz, dx in OFFSETS:
            if dx in X_ORDER[half * 2 : half * 2 + 2]:
                disp_copy(dz, dx).start()
    for m in range(3):
        sib_copy(0, m, core).start()

    received[place_of(0, 0), :] = outgoing[slots_of(0, 0), :]

    loads[3].wait()
    gate = jnp.zeros((NEP, TOK), jnp.float32)
    for k in range(TOPK):
        hit = routes_t[k : k + 1, :] == owner_expert
        gate = gate + jnp.where(hit, gates_t[k : k + 1, :], 0.0)
    spread = jnp.where(taken, jnp.broadcast_to(gate[:, None, :], (NEP, CAP, TOK)), 0.0)
    spread = spread.reshape(SLOTS, TOK).T
    high = spread.astype(jnp.bfloat16)
    gate_hi[...] = high
    gate_lo[...] = (spread - high.astype(jnp.float32)).astype(jnp.bfloat16)

    def ring_turn(step, matrices):
        for m in matrices:
            for direction in range(2):
                ring_arrival(direction, step, m).wait_recv()
                if step < NY // 2:
                    ring_copy(direction, step + 1, m).start()
                sib_copy(1 + direction * (NY // 2) + step - 1, m, core).start()

    ring_turn(1, (0, 1))
    for direction in range(2):
        ring_copy(direction, 1, 2).start()
    for d in range(1, NZ):
        pz_copy(d, arrives=True).wait_recv()
    for d in range(1, NX):
        px_copy(d).start()
    ring_turn(2, (0, 1))
    ring_turn(1, (2,))
    ring_turn(3, (0, 1))
    ring_turn(2, (2,))
    ring_turn(4, (0, 1))
    ring_turn(3, (2,))

    def partners(half):
        return [
            (dz, dx)
            for dz in Z_ORDER
            for dx in X_ORDER[half * 2 : half * 2 + 2]
            if (dz, dx) != (0, 0)
        ]

    def up(half):
        span = slice(half * HALF, (half + 1) * HALF)
        for dz, dx in partners(half):
            disp_copy(-dz % NZ, -dx % NX).wait_recv()
        for n in range(FF // 256):
            at = slice(n * 256, (n + 1) * 256)
            gated = jnp.dot(
                received[span, :], weights[0, :, at], preferred_element_type=jnp.float32
            )
            raised = jnp.dot(
                received[span, :], weights[1, :, at], preferred_element_type=jnp.float32
            )
            hidden[span, at] = (gated / (1.0 + jnp.exp(-gated)) * raised).astype(jnp.bfloat16)

    def down(half, group):
        span = slice(half * HALF, (half + 1) * HALF)
        for n in range(*GROUPS[group]):
            rows = pl.ds(pl.multiple_of(ys[Y_ORDER[n]] * 256, 256), 256)
            produced[span, n * 256 : (n + 1) * 256] = lax.dot_general(
                hidden[span, :], weights[2, rows, :], (((1,), (1,)), ((), ())),
                preferred_element_type=jnp.float32,
            ).astype(jnp.bfloat16)
        for dz, dx in partners(half):
            ret_copy(dz, dx, group).start()

    def sib_wait(m, kinds):
        for kind in kinds:
            sib_copy(kind, m, 1 - core).wait_recv()

    for load in loads[6:]:
        load.wait()
    for m in range(2):
        sib_wait(m, range(1 + NY))
    up(0)
    ring_turn(4, (2,))
    sib_wait(2, (0, 1, 2, 5, 6))
    down(0, 0)
    up(1)
    down(1, 0)
    sib_wait(2, (3, 4, 7, 8))
    down(0, 1)
    down(1, 1)

    returned[slots_of(0, 0), :] = produced[place_of(0, 0), :]

    for d in range(1, NX):
        px_copy(d, arrives=True).wait_recv()

    @pl.loop(0, NEP // 2)
    def _(i):
        first = prompt_buf[i // 4, (i % 4) * 2].astype(jnp.float32)
        second = prompt_buf[i // 4, (i % 4) * 2 + 1].astype(jnp.float32)
        at = pl.ds(pl.multiple_of(i * 2 * PROMPT_ROWS, 2 * PROMPT_ROWS), 2 * PROMPT_ROWS)
        keys[at, :] = jnp.concatenate(
            [first[:PROMPT_ROWS], second[:PROMPT_ROWS]], axis=0
        ).astype(jnp.bfloat16)
        values[at, :] = jnp.concatenate(
            [first[PROMPT_ROWS:], second[PROMPT_ROWS:]], axis=0
        ).astype(jnp.bfloat16)

    causal = lax.broadcasted_iota(jnp.int32, (TOK, TOK), 1) <= lax.broadcasted_iota(
        jnp.int32, (TOK, TOK), 0
    )
    loads[4].wait()
    loads[5].wait()

    @pl.loop(0, HQ, unroll=2)
    def _(head):
        at = pl.ds(pl.multiple_of(head * HD, HD), HD)
        kv = pl.ds(pl.multiple_of((head // (HQ // KVH)) * HD, HD), HD)
        kv_value = pl.ds(pl.multiple_of(KVH * HD + (head // (HQ // KVH)) * HD, HD), HD)
        query = q_buf[:, at]
        contract = (((1,), (1,)), ((), ()))
        shared = lax.dot_general(
            query, keys[:, kv], contract, preferred_element_type=jnp.float32
        )
        own = lax.dot_general(
            query, resp_kv[:, kv], contract, preferred_element_type=jnp.float32
        )
        own = jnp.where(causal, own, -jnp.inf)
        top = jnp.maximum(
            jnp.max(shared, axis=-1, keepdims=True), jnp.max(own, axis=-1, keepdims=True)
        )
        shared = jnp.exp((shared - top) * SCALE)
        own = jnp.exp((own - top) * SCALE)
        denominator = jnp.sum(shared, axis=-1, keepdims=True) + jnp.sum(
            own, axis=-1, keepdims=True
        )
        summed = jnp.dot(
            shared.astype(jnp.bfloat16), values[:, kv], preferred_element_type=jnp.float32
        ) + jnp.dot(
            own.astype(jnp.bfloat16), resp_kv[:, kv_value], preferred_element_type=jnp.float32
        )
        ctx_buf[:, at] = (summed / denominator).astype(jnp.bfloat16)

    ctx_copy = pltpu.make_async_copy(ctx_buf, ctx_hbm, local_sem.at[9])
    ctx_copy.start()

    for m in range(3):
        for direction in range(2):
            for step in range(1, NY // 2 + 1):
                ring_copy(direction, step, m).wait_send()
        for kind in range(1 + NY):
            sib_copy(kind, m, core).wait_send()
    for d in range(1, NZ):
        pz_copy(d).wait_send()
    for d in range(1, NX):
        px_copy(d).wait_send()
    for dz, dx in OFFSETS:
        disp_copy(dz, dx).wait_send()

    ctx_copy.wait()
    for group in range(len(GROUPS)):
        for dz, dx in OFFSETS:
            ret_copy(dz, dx, group).wait_send()
        for dz, dx in OFFSETS:
            ret_copy(dz, dx, group).wait_recv()
        for n in range(*GROUPS[group]):
            at = slice(n * 256, (n + 1) * 256)
            columns = pl.ds(pl.multiple_of(ys[Y_ORDER[n]] * 256, 256), 256)
            moe_out[:, columns] = (
                jnp.dot(gate_hi[...], returned[:, at], preferred_element_type=jnp.float32)
                + jnp.dot(gate_lo[...], returned[:, at], preferred_element_type=jnp.float32)
            ).astype(jnp.bfloat16)


def publish_kernel(ctx, moe, ctx_out, moe_out, ctx_buf, moe_buf, in_sem, out_sem):
    pieces = [(ctx, ctx_buf, ctx_out, i, TOK // 4) for i in range(4)]
    pieces += [(moe, moe_buf, moe_out, i, TOK // 2) for i in range(2)]
    incoming, outgoing = [], []
    for n, (src, buf, dst, i, rows) in enumerate(pieces):
        at = slice(i * rows, (i + 1) * rows)
        incoming.append(pltpu.make_async_copy(src.at[at], buf.at[at], in_sem.at[n]))
        outgoing.append(pltpu.make_async_copy(buf.at[at], dst.at[at], out_sem.at[n]))
    for copy in incoming:
        copy.start()
    for copy, following in zip(incoming, outgoing):
        copy.wait()
        following.start()
    for copy in outgoing:
        copy.wait()


def publish(ctx, moe):
    anywhere = pl.BlockSpec(memory_space=pl.ANY)
    return pl.pallas_call(
        publish_kernel,
        out_shape=tuple(jax.ShapeDtypeStruct(a.shape, a.dtype) for a in (ctx, moe)),
        in_specs=[anywhere] * 2,
        out_specs=(anywhere,) * 2,
        scratch_shapes=[
            pltpu.VMEM(ctx.shape, ctx.dtype),
            pltpu.VMEM(moe.shape, moe.dtype),
            pltpu.SemaphoreType.DMA((6,)),
            pltpu.SemaphoreType.DMA((6,)),
        ],
        compiler_params=pltpu.CompilerParams(vmem_limit_bytes=VMEM_LIMIT),
    )(ctx, moe)


def body(resp_q, resp_kv, prompt_kv, moe_in, routes, gate_probs, w_gate, w_up, w_down):
    vmem = pl.BlockSpec(memory_space=pltpu.VMEM)
    anywhere = pl.BlockSpec(memory_space=pl.ANY)
    bf16 = jnp.bfloat16
    dma = pltpu.SemaphoreType.DMA
    results = pl.pallas_call(
        layer_kernel,
        out_shape=(
            jax.ShapeDtypeStruct((TOK, HQ * HD), bf16),
            jax.ShapeDtypeStruct((TOK, D), bf16),
        ),
        in_specs=[anywhere] * 9,
        out_specs=(anywhere, vmem),
        scratch_shapes=[
            pltpu.VMEM((3, D, FF), bf16),
            pltpu.VMEM((SLOTS, D), bf16),
            pltpu.VMEM((SLOTS, D), bf16),
            pltpu.VMEM((SLOTS, FF), bf16),
            pltpu.VMEM((SLOTS, D), bf16),
            pltpu.VMEM((SLOTS, D), bf16),
            pltpu.VMEM((TOK, SLOTS), bf16),
            pltpu.VMEM((TOK, SLOTS), bf16),
            pltpu.VMEM((TOK, HQ * HD), bf16),
            pltpu.VMEM((TOK, HQ * HD), bf16),
            pltpu.VMEM((NX, NZ, 2 * PROMPT_ROWS, KVH * HD), bf16),
            pltpu.VMEM((NEP * PROMPT_ROWS, KVH * HD), bf16),
            pltpu.VMEM((NEP * PROMPT_ROWS, KVH * HD), bf16),
            pltpu.VMEM((TOK, 2 * KVH * HD), bf16),
            pltpu.VMEM((PROMPT_ROWS, 2 * KVH * HD), bf16),
            pltpu.VMEM((TOK, D), bf16),
            pltpu.VMEM((TOPK, TOK), jnp.int32),
            pltpu.VMEM((TOPK, TOK), jnp.float32),
            dma((10,)),
            dma((2, NY // 2, 3)),
            dma((2, NY // 2, 3)),
            dma((1 + NY, 3)),
            dma((1 + NY, 3)),
            dma((NZ - 1,)),
            dma((NZ - 1,)),
            dma((NX - 1,)),
            dma((NX - 1,)),
            dma((NEP,)),
            dma((NEP,)),
            dma((len(GROUPS), NEP)),
            dma((len(GROUPS), NEP)),
        ],
        compiler_params=pltpu.CompilerParams(
            collective_id=0, has_side_effects=True, vmem_limit_bytes=VMEM_LIMIT
        ),
        cost_estimate=pl.CostEstimate(
            flops=7_000_000_000, bytes_accessed=6_000_000, transcendentals=4_000_000
        ),
    )(
        resp_q, resp_kv, prompt_kv, moe_in, routes.T, gate_probs.T,
        w_gate[0], w_up[0], w_down[0],
    )
    return publish(*results)


def solution(mesh):
    placed = P(("grp", "ep"), None)
    weight = P("ep", "grp", None)
    return jax.shard_map(
        body,
        mesh=mesh,
        in_specs=(placed,) * 6 + (weight,) * 3,
        out_specs=(placed, placed),
        check_vma=False,
    )
```

time: 236 us -> 119 us (0.50)
  the two profiles are of different devices: /device:TPU:5 before, /device:TPU:2 now
where the time goes in v2:
time: 119 us; the launch traced here: 118 us
  Pallas kernels  118 us (99%)
    pallas_call x1, Pallas kernels, body(): pl.pallas_call(layer_kernel, out_shape=(jax.ShapeDtypeStruct((TOK, HQ * H...  116 us

profile of v2, /device:TPU:2, one launch (start us, length us, event | category | flops | bytes accessed | tf_op | source)
XLA Modules:
  0.0 118.5 jit_solution(5604933931385117110)
XLA Ops:
  0.6 115.7 %shard_map.104 = (bf16[128,4096]{1,0:T(8,128)(2,1)}, bf16[128,2048]{1,0:T(8,128)(2,1)}) custom-call(bf16[128,4096]{1,0:T(8,128)(2,1)} %q_hbm.1, bf16[128,512]{1,0:T(8,128)(2,1)} %resp_hbm.1, bf16[24,512]{1,0:T(8,128)(2,1)} %prompt_hbm.1, bf16[128,2048]{1,0:T(8,128)(2,1)} %moe_hbm.1, s32[8,128]{1,0:T(8,128)} %bitcast.8, f32[8,128]{1,0:T(8,128)} %bitcast.9, ...), custom_call_target="tpu_custom_call" | custom-call | flops 7000000000 | bytes 6000000 | tf_op jit(solution)/shard_map/pallas_call | solution.py:415
  116.3 2.2 %shard_map.105 = (bf16[128,4096]{1,0:T(8,128)(2,1)}, bf16[128,2048]{1,0:T(8,128)(2,1)}) custom-call(bf16[128,4096]{1,0:T(8,128)(2,1)} %get-tuple-element.4.ctx, bf16[128,2048]{1,0:T(8,128)(2,1)} %get-tuple-element.5.moe), custom_call_target="tpu_custom_call" | custom-call | tf_op jit(solution)/shard_map/pallas_call | solution.py:395

commit v3 on v2

--- a/solution.py
+++ b/solution.py
@@ -30,6 +30,7 @@
 X_ORDER = (0, 2, 1, 3)
 Y_ORDER = (0, 1, 7, 2, 6, 3, 5, 4)
 GROUPS = ((0, 5), (5, 8))
+LAST_ORDER = (0, 1, 5, 2, 6, 3, 7, 4)
 
 
 def layer_kernel(
@@ -55,6 +56,12 @@
     def in_plane(dz, dx):
         return (grp, zs[dz] * NX + xs[dx])
 
+    barrier = pltpu.get_barrier_semaphore()
+    for dz, dx in reversed(OFFSETS):
+        pl.semaphore_signal(barrier, inc=1, device_id=in_plane(dz, dx), device_id_type=MESH)
+    for other in (sibling, right, left):
+        pl.semaphore_signal(barrier, inc=1, device_id=(other, ep), device_id_type=MESH)
+
     loads = [
         pltpu.make_async_copy(src, dst, local_sem.at[i])
         for i, (src, dst) in enumerate(
@@ -68,11 +75,6 @@
     for load in loads[:4]:
         load.start()
 
-    barrier = pltpu.get_barrier_semaphore()
-    for other in (sibling, right, left):
-        pl.semaphore_signal(barrier, inc=1, device_id=(other, ep), device_id_type=MESH)
-    for dz, dx in OFFSETS:
-        pl.semaphore_signal(barrier, inc=1, device_id=in_plane(dz, dx), device_id_type=MESH)
     for load in loads[4:]:
         load.start()
 
@@ -195,12 +197,12 @@
     for m in range(2):
         for direction in range(2):
             ring_copy(direction, 1, m).start()
-    for d in range(1, NZ):
-        pz_copy(d).start()
     for half in range(2):
         for dz, dx in OFFSETS:
             if dx in X_ORDER[half * 2 : half * 2 + 2]:
                 disp_copy(dz, dx).start()
+    for d in range(1, NZ):
+        pz_copy(d).start()
     for m in range(3):
         sib_copy(0, m, core).start()
 
@@ -228,10 +230,6 @@
     ring_turn(1, (0, 1))
     for direction in range(2):
         ring_copy(direction, 1, 2).start()
-    for d in range(1, NZ):
-        pz_copy(d, arrives=True).wait_recv()
-    for d in range(1, NX):
-        px_copy(d).start()
     ring_turn(2, (0, 1))
     ring_turn(1, (2,))
     ring_turn(3, (0, 1))
@@ -269,8 +267,37 @@
                 hidden[span, :], weights[2, rows, :], (((1,), (1,)), ((), ())),
                 preferred_element_type=jnp.float32,
             ).astype(jnp.bfloat16)
+
+    def give_back(half, group):
         for dz, dx in partners(half):
             ret_copy(dz, dx, group).start()
+
+    def give_back_by_z(group):
+        for target in LAST_ORDER:
+            dz = lax.rem(target - z + NZ, NZ)
+            for dx in X_ORDER:
+                copy = pltpu.make_async_remote_copy(
+                    src_ref=produced.at[
+                        pl.ds(pl.multiple_of((X_ORDER.index(dx) * NZ + dz) * CAP, CAP), CAP),
+                        slice(256 * GROUPS[group][0], 256 * GROUPS[group][1]),
+                    ],
+                    dst_ref=returned.at[
+                        pl.ds(
+                            pl.multiple_of(
+                                (lax.rem(NZ - dz, NZ) * NX + (-dx % NX)) * CAP, CAP
+                            ),
+                            CAP,
+                        ),
+                        slice(256 * GROUPS[group][0], 256 * GROUPS[group][1]),
+                    ],
+                    send_sem=ret_send.at[group, dz * NX + dx],
+                    recv_sem=ret_recv.at[group, dz * NX + dx],
+                    device_id=(grp, target * NX + xs[dx]), device_id_type=MESH,
+                )
+                if dx == 0:
+                    pl.when(target != z)(copy.start)
+                else:
+                    copy.start()
 
     def sib_wait(m, kinds):
         for kind in kinds:
@@ -284,14 +311,21 @@
     ring_turn(4, (2,))
     sib_wait(2, (0, 1, 2, 5, 6))
     down(0, 0)
+    give_back(0, 0)
     up(1)
     down(1, 0)
+    give_back(1, 0)
     sib_wait(2, (3, 4, 7, 8))
     down(0, 1)
     down(1, 1)
+    give_back_by_z(1)
 
     returned[slots_of(0, 0), :] = produced[place_of(0, 0), :]
 
+    for d in range(1, NZ):
+        pz_copy(d, arrives=True).wait_recv()
+    for d in range(1, NX):
+        px_copy(d).start()
     for d in range(1, NX):
         px_copy(d, arrives=True).wait_recv()
 

time: 119 us -> 116 us (0.975)
  the two profiles are of different devices: /device:TPU:2 before, /device:TPU:128 now
where the time goes in v3:
time: 116 us; the launch traced here: 115 us
  Pallas kernels  115 us (99%)
    pallas_call x1, Pallas kernels, body(): pl.pallas_call(layer_kernel, out_shape=(jax.ShapeDtypeStruct((TOK, HQ * H...  113 us

profile of v3, /device:TPU:128, one launch (start us, length us, event | category | flops | bytes accessed | tf_op | source)
XLA Modules:
  0.0 115.4 jit_solution(9078777336099951337)
XLA Ops:
  0.6 112.6 %shard_map.104 = (bf16[128,4096]{1,0:T(8,128)(2,1)}, bf16[128,2048]{1,0:T(8,128)(2,1)}) custom-call(bf16[128,4096]{1,0:T(8,128)(2,1)} %q_hbm.1, bf16[128,512]{1,0:T(8,128)(2,1)} %resp_hbm.1, bf16[24,512]{1,0:T(8,128)(2,1)} %prompt_hbm.1, bf16[128,2048]{1,0:T(8,128)(2,1)} %moe_hbm.1, s32[8,128]{1,0:T(8,128)} %bitcast.8, f32[8,128]{1,0:T(8,128)} %bitcast.9, ...), custom_call_target="tpu_custom_call" | custom-call | flops 7000000000 | bytes 6000000 | tf_op jit(solution)/shard_map/pallas_call | solution.py:449
  113.2 2.2 %shard_map.105 = (bf16[128,4096]{1,0:T(8,128)(2,1)}, bf16[128,2048]{1,0:T(8,128)(2,1)}) custom-call(bf16[128,4096]{1,0:T(8,128)(2,1)} %get-tuple-element.4.ctx, bf16[128,2048]{1,0:T(8,128)(2,1)} %get-tuple-element.5.moe), custom_call_target="tpu_custom_call" | custom-call | tf_op jit(solution)/shard_map/pallas_call | solution.py:429

commit v4 on v3

--- a/solution.py
+++ b/solution.py
@@ -35,9 +35,9 @@
 
 def layer_kernel(
     q_hbm, resp_hbm, prompt_hbm, moe_hbm, routes_hbm, gates_hbm, wg_hbm, wu_hbm, wd_hbm,
-    ctx_hbm, moe_out,
+    ctx_hbm, moe_hbm_out,
     weights, outgoing, received, hidden, produced, returned, gate_hi, gate_lo,
-    q_buf, ctx_buf, prompt_buf, keys, values, resp_kv, prompt_kv, moe_in, routes_t, gates_t,
+    q_buf, ctx_buf, prompt_buf, keys, values, resp_kv, prompt_kv, moe_in, routes_t, gates_t, moe_out,
     local_sem, ring_send, ring_recv, sib_send, sib_recv, pz_send, pz_recv, px_send, px_recv,
     disp_send, disp_recv, ret_send, ret_recv,
 ):
@@ -235,7 +235,6 @@
     ring_turn(3, (0, 1))
     ring_turn(2, (2,))
     ring_turn(4, (0, 1))
-    ring_turn(3, (2,))
 
     def partners(half):
         return [
@@ -308,13 +307,14 @@
     for m in range(2):
         sib_wait(m, range(1 + NY))
     up(0)
-    ring_turn(4, (2,))
     sib_wait(2, (0, 1, 2, 5, 6))
     down(0, 0)
     give_back(0, 0)
+    ring_turn(3, (2,))
     up(1)
     down(1, 0)
     give_back(1, 0)
+    ring_turn(4, (2,))
     sib_wait(2, (3, 4, 7, 8))
     down(0, 1)
     down(1, 1)
@@ -392,6 +392,12 @@
     for dz, dx in OFFSETS:
         disp_copy(dz, dx).wait_send()
 
+    def moe_copy(n):
+        columns = pl.ds(pl.multiple_of(ys[Y_ORDER[n]] * 256, 256), 256)
+        return pltpu.make_async_copy(
+            moe_out.at[:, n * 256 : (n + 1) * 256], moe_hbm_out.at[:, columns], local_sem.at[10 + n]
+        )
+
     ctx_copy.wait()
     for group in range(len(GROUPS)):
         for dz, dx in OFFSETS:
@@ -400,11 +406,13 @@
             ret_copy(dz, dx, group).wait_recv()
         for n in range(*GROUPS[group]):
             at = slice(n * 256, (n + 1) * 256)
-            columns = pl.ds(pl.multiple_of(ys[Y_ORDER[n]] * 256, 256), 256)
-            moe_out[:, columns] = (
+            moe_out[:, at] = (
                 jnp.dot(gate_hi[...], returned[:, at], preferred_element_type=jnp.float32)
                 + jnp.dot(gate_lo[...], returned[:, at], preferred_element_type=jnp.float32)
             ).astype(jnp.bfloat16)
+            moe_copy(n).start()
+    for n in range(NY):
+        moe_copy(n).wait()
 
 
 def publish_kernel(ctx, moe, ctx_out, moe_out, ctx_buf, moe_buf, in_sem, out_sem):
@@ -442,7 +450,6 @@
 
 
 def body(resp_q, resp_kv, prompt_kv, moe_in, routes, gate_probs, w_gate, w_up, w_down):
-    vmem = pl.BlockSpec(memory_space=pltpu.VMEM)
     anywhere = pl.BlockSpec(memory_space=pl.ANY)
     bf16 = jnp.bfloat16
     dma = pltpu.SemaphoreType.DMA
@@ -453,7 +460,7 @@
             jax.ShapeDtypeStruct((TOK, D), bf16),
         ),
         in_specs=[anywhere] * 9,
-        out_specs=(anywhere, vmem),
+        out_specs=(anywhere, anywhere),
         scratch_shapes=[
             pltpu.VMEM((3, D, FF), bf16),
             pltpu.VMEM((SLOTS, D), bf16),
@@ -473,7 +480,8 @@
             pltpu.VMEM((TOK, D), bf16),
             pltpu.VMEM((TOPK, TOK), jnp.int32),
             pltpu.VMEM((TOPK, TOK), jnp.float32),
-            dma((10,)),
+            pltpu.VMEM((TOK, D), bf16),
+            dma((10 + NY,)),
             dma((2, NY // 2, 3)),
             dma((2, NY // 2, 3)),
             dma((1 + NY, 3)),

time: 116 us -> 115 us (level)
  no operation moved by 1% of the time
where the time goes in v4:
time: 115 us
  Pallas kernels  114 us (99%)
    pallas_call x1, Pallas kernels, body(): pl.pallas_call(layer_kernel, out_shape=(jax.ShapeDtypeStruct((TOK, HQ * H...  112 us

profile of v4, /device:TPU:128, one launch (start us, length us, event | category | flops | bytes accessed | tf_op | source)
XLA Modules:
  0.0 115.1 jit_solution(3939955493565250182)
XLA Ops:
  0.6 112.3 %shard_map.104 = (bf16[128,4096]{1,0:T(8,128)(2,1)}, bf16[128,2048]{1,0:T(8,128)(2,1)}) custom-call(bf16[128,4096]{1,0:T(8,128)(2,1)} %q_hbm.1, bf16[128,512]{1,0:T(8,128)(2,1)} %resp_hbm.1, bf16[24,512]{1,0:T(8,128)(2,1)} %prompt_hbm.1, bf16[128,2048]{1,0:T(8,128)(2,1)} %moe_hbm.1, s32[8,128]{1,0:T(8,128)} %bitcast.8, f32[8,128]{1,0:T(8,128)} %bitcast.9, ...), custom_call_target="tpu_custom_call" | custom-call | flops 7000000000 | bytes 6000000 | tf_op jit(solution)/shard_map/pallas_call | solution.py:456
  112.9 2.2 %shard_map.105 = (bf16[128,4096]{1,0:T(8,128)(2,1)}, bf16[128,2048]{1,0:T(8,128)(2,1)}) custom-call(bf16[128,4096]{1,0:T(8,128)(2,1)} %get-tuple-element.4.ctx, bf16[128,2048]{1,0:T(8,128)(2,1)} %get-tuple-element.5.moe), custom_call_target="tpu_custom_call" | custom-call | tf_op jit(solution)/shard_map/pallas_call | solution.py:437

commit v5 on v3

--- a/solution.py
+++ b/solution.py
@@ -30,7 +30,7 @@
 X_ORDER = (0, 2, 1, 3)
 Y_ORDER = (0, 1, 7, 2, 6, 3, 5, 4)
 GROUPS = ((0, 5), (5, 8))
-LAST_ORDER = (0, 1, 5, 2, 6, 3, 7, 4)
+LAST_ORDER = (0, 4, 1, 5, 2, 6, 3, 7)
 
 
 def layer_kernel(
@@ -235,7 +235,6 @@
     ring_turn(3, (0, 1))
     ring_turn(2, (2,))
     ring_turn(4, (0, 1))
-    ring_turn(3, (2,))
 
     def partners(half):
         return [
@@ -308,13 +307,14 @@
     for m in range(2):
         sib_wait(m, range(1 + NY))
     up(0)
-    ring_turn(4, (2,))
     sib_wait(2, (0, 1, 2, 5, 6))
     down(0, 0)
     give_back(0, 0)
+    ring_turn(3, (2,))
     up(1)
     down(1, 0)
     give_back(1, 0)
+    ring_turn(4, (2,))
     sib_wait(2, (3, 4, 7, 8))
     down(0, 1)
     down(1, 1)

time: 116 us -> 115 us (level)
  no operation moved by 1% of the time
where the time goes in v5:
time: 115 us
  Pallas kernels  115 us (100%)
    pallas_call x1, Pallas kernels, body(): pl.pallas_call(layer_kernel, out_shape=(jax.ShapeDtypeStruct((TOK, HQ * H...  112 us

profile of v5, /device:TPU:128, one launch (start us, length us, event | category | flops | bytes accessed | tf_op | source)
XLA Modules:
  0.0 115.2 jit_solution(254665441851410005)
XLA Ops:
  0.6 112.4 %shard_map.104 = (bf16[128,4096]{1,0:T(8,128)(2,1)}, bf16[128,2048]{1,0:T(8,128)(2,1)}) custom-call(bf16[128,4096]{1,0:T(8,128)(2,1)} %q_hbm.1, bf16[128,512]{1,0:T(8,128)(2,1)} %resp_hbm.1, bf16[24,512]{1,0:T(8,128)(2,1)} %prompt_hbm.1, bf16[128,2048]{1,0:T(8,128)(2,1)} %moe_hbm.1, s32[8,128]{1,0:T(8,128)} %bitcast.8, f32[8,128]{1,0:T(8,128)} %bitcast.9, ...), custom_call_target="tpu_custom_call" | custom-call | flops 7000000000 | bytes 6000000 | tf_op jit(solution)/shard_map/pallas_call | solution.py:449
  113.0 2.2 %shard_map.105 = (bf16[128,4096]{1,0:T(8,128)(2,1)}, bf16[128,2048]{1,0:T(8,128)(2,1)}) custom-call(bf16[128,4096]{1,0:T(8,128)(2,1)} %get-tuple-element.4.ctx, bf16[128,2048]{1,0:T(8,128)(2,1)} %get-tuple-element.5.moe), custom_call_target="tpu_custom_call" | custom-call | tf_op jit(solution)/shard_map/pallas_call | solution.py:429
